TPU v7x, 32 devices: a whole 2x2x4 slice. The times are simulated.
32 devices in a mesh: row: 4 (over y, x), col: 8 (over z, core).
Axes of the slice: x: 2, y: 2, z: 4, core: 2. Of those that a mesh axis runs over, the one named last changes fastest.
Arguments:
- diag_blocks: float32 [2, 512, 512], replicated, may hold values from -1 to 5, as said below
- pivot_flags: int32 [2, 512], replicated, may hold values 0 or 1
- panels: bfloat16 [2, 8192, 512], P(None, ('row', 'col')), may hold values from -3 to 3
- structure: int32 [2, 8192], P(None, ('row', 'col')), may hold values 0 or 1
- ancestor_inverse: bfloat16 [8192, 8192], P('row', 'col'), may hold values from -0.09375 to 0.09375
Outputs:
- inverse_panel: bfloat16 [2, 8192, 512], P(None, ('row', 'col'))
- inverse_diagonal: float32 [2, 512, 512], replicated
Inputs may be any that keep to these rules, and one draw needn't show every extreme that they name: Each diag_blocks[k] is symmetric, and its off-diagonal part is small enough that every eigenvalue of each shifted block is at least 0.8, so every shifted block is positive definite.
All inputs are finite; a program needn't handle non-finite values. No bound on the sum of `structure` on one device may be relied on, other than what follows from the above.
Results may differ from a plain program's by a relative error of at most 0.0051.
Values may be sent and summed in bfloat16 or wider, within the bound.
A program may use at most 192 MiB of HBM per device.

v0:
```python
import jax
import jax.numpy as jnp
from jax import lax
from jax.sharding import PartitionSpec as P

HIGHEST_PRECISION = lax.Precision.HIGHEST
PERTURBATION = 1.0


def from_root(value, axis, source):
    kept = jnp.where(lax.axis_index(axis) == source, value, 0).astype(value.dtype)
    return lax.psum(kept, axis)


def factor_inverse(diagonal_block, flag_row):
    node_width = diagonal_block.shape[0]
    identity = jnp.eye(node_width, dtype=jnp.float32)
    shifted = diagonal_block + PERTURBATION * identity * flag_row.astype(jnp.float32)[None, :]
    factor_lower = jnp.linalg.cholesky(shifted)
    lower_inverse = jax.scipy.linalg.solve_triangular(factor_lower, identity, lower=True)
    return jnp.dot(lower_inverse.T, lower_inverse, precision=HIGHEST_PRECISION)


def normalize_panel(panel_rows, member_row, inverse):
    masked = panel_rows.astype(jnp.float32) * member_row.astype(jnp.float32)[:, None]
    return jnp.dot(masked, inverse, precision=HIGHEST_PRECISION).astype(jnp.bfloat16)


def exact_contract(left_rows, right_rows):
    dims = (((0,), (0,)), ((), ()))
    return lax.dot_general(
        left_rows.astype(jnp.float32),
        right_rows,
        dims,
        precision=HIGHEST_PRECISION,
        preferred_element_type=jnp.float32,
    )


def local(diag_blocks, pivot_flags, panels, structure, ancestor_inverse):
    node_count = diag_blocks.shape[0]
    inverses = [
        factor_inverse(diag_blocks[supernode], pivot_flags[supernode])
        for supernode in range(node_count)
    ]
    normed = [
        normalize_panel(panels[supernode], structure[supernode], inverses[supernode])
        for supernode in range(node_count)
    ]
    col_ratio = lax.axis_size("col") // lax.axis_size("row")
    col_index = lax.axis_index("col")
    own_rows = ancestor_inverse.shape[0] // lax.axis_size("col")
    panel_terms = []
    diagonal_terms = []
    for panel_group in normed:
        row_block = lax.all_gather(panel_group, "col", axis=0, tiled=True)
        block_rows = row_block.shape[0] // col_ratio
        column_part = lax.dynamic_slice_in_dim(
            row_block, col_index % col_ratio * block_rows, block_rows, 0
        )
        column_block = from_root(column_part, "row", col_index // col_ratio)

        def product(offset, row_count, column_block=column_block):
            return jnp.dot(ancestor_inverse, column_block, preferred_element_type=jnp.float32)

        summed = lax.psum_scatter(
            product(jnp.int32(0), own_rows * lax.axis_size("col")),
            "col",
            scatter_dimension=0,
            tiled=True,
        )
        diagonal_terms.append(exact_contract(panel_group, summed))
        panel_terms.append(summed)
    totals = lax.psum(jnp.stack(diagonal_terms), ("row", "col"))
    inverse_diagonal = jnp.stack(inverses) + totals
    inverse_panel = (-jnp.stack(panel_terms)).astype(jnp.bfloat16)
    return (inverse_panel, inverse_diagonal)


def solution(mesh):
    in_specs = (P(), P(), P(None, ("row", "col"), None), P(None, ("row", "col")), P("row", "col"))
    out_specs = (P(None, ("row", "col"), None), P())
    return jax.shard_map(local, mesh=mesh, in_specs=in_specs, out_specs=out_specs, check_vma=False)
```

profile of v0, /device:TPU:0, one launch (start us, length us, event | category | flops | bytes accessed | tf_op | source)
XLA Modules:
  0.0 663.8 jit_solution(1565190489464110326)
XLA Ops:
  7.3 2.7 fusion.88
  12.2 1.5 fusion.17
  13.7 11.7 %cholesky.358 = f32[128,128]{1,0:T(8,128)S(1)} custom-call(f32[128,128]{1,0:T(8,128)S(1)} %cholesky.439), custom_call_target="Cholesky" | custom-call | tf_op jit(solution)/shard_map/jit(cholesky)/cholesky | solution.py:19
  25.6 9.8 %custom-call.31 = f32[1,128,128]{1,2,0:T(8,128)S(1)} custom-call(f32[1,128,128]{2,1,0:T(8,128)S(1)} %get-tuple-element.65), custom_call_target="InvertDiagBlocksLowerTriangular" | custom-call | tf_op jit(solution)/shard_map/jit(cholesky)/cholesky | solution.py:19
  36.1 11.7 %cholesky.377 = f32[128,128]{1,0:T(8,128)S(1)} custom-call(f32[128,128]{1,0:T(8,128)S(1)} %cholesky.443), custom_call_target="Cholesky" | custom-call | tf_op jit(solution)/shard_map/jit(cholesky)/cholesky | solution.py:19
  47.8 9.9 %custom-call.32 = f32[1,128,128]{1,2,0:T(8,128)S(1)} custom-call(f32[1,128,128]{2,1,0:T(8,128)S(1)} %get-tuple-element.62), custom_call_target="InvertDiagBlocksLowerTriangular" | custom-call | tf_op jit(solution)/shard_map/jit(cholesky)/cholesky | solution.py:19
  58.4 11.7 %cholesky.398 = f32[128,128]{1,0:T(8,128)S(1)} custom-call(f32[128,128]{1,0:T(8,128)S(1)} %cholesky.448), custom_call_target="Cholesky" | custom-call | tf_op jit(solution)/shard_map/jit(cholesky)/cholesky | solution.py:19
  70.2 9.8 %custom-call.33 = f32[1,128,128]{1,2,0:T(8,128)S(1)} custom-call(f32[1,128,128]{2,1,0:T(8,128)S(1)} %get-tuple-element.59), custom_call_target="InvertDiagBlocksLowerTriangular" | custom-call | tf_op jit(solution)/shard_map/jit(cholesky)/cholesky | solution.py:19
  80.6 11.9 %cholesky.415 = f32[128,128]{1,0:T(8,128)S(1)} custom-call(f32[128,128]{1,0:T(8,128)S(1)} %convolution_subtract_fusion.10), custom_call_target="Cholesky" | custom-call | tf_op jit(solution)/shard_map/jit(cholesky)/cholesky | solution.py:19
  97.3 8.1 %while.5 = (s32[]{:T(128)}, f32[512,512]{1,0:T(8,128)S(1)}, s32[4,2]{0,1:T(2,128)S(1)}, f32[4,128,128]{2,1,0:T(8,128)S(1)}, s32[]{:T(128)}) while((s32[]{:T(128)}, f32[512,512]{1,0:T(8,128)S(1)}, s32[4,2]{0,1:T(2,128)S(1)}, f32[4,128,128]{2,1,0:T(8,128)S(1)}, s32[]{:T(128)}) %tuple.60), condition=%wide.while_cond.clone, body=%wide.while_body.clone.sunk | while | flops 2 | bytes 131189 | solution.py:20
  98.0 1.3 bitcast_dynamic-update-slice_fusion.5
  100.0 1.3 bitcast_dynamic-update-slice_fusion.5
  102.0 1.3 bitcast_dynamic-update-slice_fusion.5
  105.4 39.3 %custom-call.34 = f32[4,128,128]{1,2,0:T(8,128)S(1)} custom-call(f32[4,128,128]{2,1,0:T(8,128)S(1)} %get-tuple-element.19), custom_call_target="InvertDiagBlocksLowerTriangular" | custom-call | tf_op jit(solution)/shard_map/jit(_solve_triangular)/triangular_solve | solution.py:20
  147.7 1.5 convolution_subtract_fusion.4
  149.6 1.9 fusion.8
  152.6 1.8 convolution_convert_fusion
  156.7 1.5 fusion.18
  159.2 11.7 %cholesky.286 = f32[128,128]{1,0:T(8,128)S(1)} custom-call(f32[128,128]{1,0:T(8,128)S(1)} %cholesky.426), custom_call_target="Cholesky" | custom-call | tf_op jit(solution)/shard_map/jit(cholesky)/cholesky | solution.py:19
  171.0 9.8 %custom-call.27 = f32[1,128,128]{1,2,0:T(8,128)S(1)} custom-call(f32[1,128,128]{2,1,0:T(8,128)S(1)} %get-tuple-element.55), custom_call_target="InvertDiagBlocksLowerTriangular" | custom-call | tf_op jit(solution)/shard_map/jit(cholesky)/cholesky | solution.py:19
  183.4 11.7 %cholesky.305 = f32[128,128]{1,0:T(8,128)S(1)} custom-call(f32[128,128]{1,0:T(8,128)S(1)} %cholesky.430), custom_call_target="Cholesky" | custom-call | tf_op jit(solution)/shard_map/jit(cholesky)/cholesky | solution.py:19
  195.1 10.0 %custom-call.28 = f32[1,128,128]{1,2,0:T(8,128)S(1)} custom-call(f32[1,128,128]{2,1,0:T(8,128)S(1)} %get-tuple-element.52), custom_call_target="InvertDiagBlocksLowerTriangular" | custom-call | tf_op jit(solution)/shard_map/jit(cholesky)/cholesky | solution.py:19
  206.7 11.7 %cholesky.326 = f32[128,128]{1,0:T(8,128)S(1)} custom-call(f32[128,128]{1,0:T(8,128)S(1)} %cholesky.435), custom_call_target="Cholesky" | custom-call | tf_op jit(solution)/shard_map/jit(cholesky)/cholesky | solution.py:19
  218.4 9.8 %custom-call.29 = f32[1,128,128]{1,2,0:T(8,128)S(1)} custom-call(f32[1,128,128]{2,1,0:T(8,128)S(1)} %get-tuple-element.49), custom_call_target="InvertDiagBlocksLowerTriangular" | custom-call | tf_op jit(solution)/shard_map/jit(cholesky)/cholesky | solution.py:19
  229.7 11.9 %cholesky.343 = f32[128,128]{1,0:T(8,128)S(1)} custom-call(f32[128,128]{1,0:T(8,128)S(1)} %convolution_subtract_fusion.11), custom_call_target="Cholesky" | custom-call | tf_op jit(solution)/shard_map/jit(cholesky)/cholesky | solution.py:19
  246.1 8.0 %while.4 = (s32[]{:T(128)}, f32[512,512]{1,0:T(8,128)S(1)}, s32[4,2]{0,1:T(2,128)S(1)}, f32[4,128,128]{2,1,0:T(8,128)S(1)}, s32[]{:T(128)}) while((s32[]{:T(128)}, f32[512,512]{1,0:T(8,128)S(1)}, s32[4,2]{0,1:T(2,128)S(1)}, f32[4,128,128]{2,1,0:T(8,128)S(1)}, s32[]{:T(128)}) %tuple.79), condition=%wide.while_cond, body=%wide.while_body.sunk | while | flops 2 | bytes 131189 | solution.py:20
  246.8 1.3 bitcast_dynamic-update-slice_fusion.4
  248.8 1.3 bitcast_dynamic-update-slice_fusion.4
  250.7 1.3 bitcast_dynamic-update-slice_fusion.4
  252.7 1.3 bitcast_dynamic-update-slice_fusion.4
  254.1 39.3 %custom-call.30 = f32[4,128,128]{1,2,0:T(8,128)S(1)} custom-call(f32[4,128,128]{2,1,0:T(8,128)S(1)} %get-tuple-element.18), custom_call_target="InvertDiagBlocksLowerTriangular" | custom-call | tf_op jit(solution)/shard_map/jit(_solve_triangular)/triangular_solve | solution.py:20
  296.3 1.5 convolution_subtract_fusion.5
  298.3 1.9 fusion
  300.2 1.8 convolution_convert_fusion.1
  302.1 2.4 dynamic-slice_select_fusion
  304.5 29.5 %all-gather.3.cloned.1.call-done = bf16[2048,512]{1,0:T(8,128)(2,1)} async-done(((bf16[256,512]{1,0:T(8,128)(2,1)}), bf16[2048,512]{1,0:T(8,128)(2,1)}) %all-gather.3.cloned.1.call-update) | async-done | bytes 2097168 | tf_op jit(solution)/shard_map/all_gather | solution.py:56
  334.0 2.4 dynamic-slice_select_fusion.1
  336.7 70.3 %all-reduce.7.cloned.1.call-done = (bf16[1024,512]{1,0:T(8,128)(2,1)}, bf16[1024,512]{1,0:T(8,128)(2,1)}) async-done(((bf16[1024,512]{1,0:T(8,128)(2,1)}, bf16[1024,512]{1,0:T(8,128)(2,1)}), (bf16[1024,512]{1,0:T(8,128)(2,1)}, bf16[1024,512]{1,0:T(8,128)(2,1)})) %all-reduce.7.cloned.1.call-update) | async-done | bytes 2097168 | tf_op jit(solution)/shard_map/psum | solution.py:12
  407.1 6.8 %convolution_bitcast_fusion = f32[2048,512]{0,1:T(8,128)} fusion(bf16[1024,512]{1,0:T(8,128)(2,1)} %get-tuple-element.38, bf16[2048,1024]{1,0:T(8,128)(2,1)} %param.12), kind=kOutput, calls=%fused_computation.4 | convolution fusion | flops 2147483648 | bytes 9437184 | tf_op jit(solution)/shard_map/dot_general | solution.py:64
  415.1 6.5 convolution_bitcast_fusion.1
  421.7 42.3 %reduce-scatter.5.cloned.1.call-done = f32[256,512]{0,1:T(8,128)} async-done(((f32[2048,512]{0,1:T(8,128)}), f32[256,512]{0,1:T(8,128)}) %reduce-scatter.5.cloned.1.call-update) | async-done | bytes 524304 | tf_op jit(solution)/shard_map/reduce_scatter | solution.py:66
  464.1 1.7 convolution_bitcast_fusion.2
  465.8 48.7 %reduce-scatter.3.cloned.1.call-done = f32[256,512]{0,1:T(8,128)} async-done(((f32[2048,512]{0,1:T(8,128)}), f32[256,512]{0,1:T(8,128)}) %reduce-scatter.3.cloned.1.call-update) | async-done | bytes 524304 | tf_op jit(solution)/shard_map/reduce_scatter | solution.py:66
  514.5 1.7 convolution_bitcast_fusion.3
  516.3 1.5 pad_maximum_fusion
  519.9 2.0 copy.11
  521.9 131.2 %all-reduce.5.cloned.1.call-done = f32[2,512,512]{2,1,0:T(8,128)} async-done(((f32[2,512,512]{2,1,0:T(8,128)}), f32[2,512,512]{2,1,0:T(8,128)}) %all-reduce.5.cloned.1.call-update) | async-done | bytes 2097168 | tf_op jit(solution)/shard_map/psum | solution.py:74
  653.1 3.4 maximum_add_fusion
  (118 shorter events, 35.6 us)
Async XLA Ops:
  7.2 295.0 %all-gather.5.cloned.1.call-start = ((), (), s32[]{:S(2)}) async-start(), calls=%async_computation.4 | async-start | bytes 2359296 | tf_op jit(solution)/shard_map/all_gather | solution.py:56
  10.0 0.7 copy-start.10
  147.6 3.9 copy-start.11
  147.7 4.9 copy-start.8
  149.6 5.3 copy-start.2
  151.5 1.1 copy-start
  154.4 179.6 %all-gather.3.cloned.1.call-start = ((), (), s32[]{:S(2)}) async-start(), calls=%async_computation.2 | async-start | bytes 2359296 | tf_op jit(solution)/shard_map/all_gather | solution.py:56
  158.2 1.0 copy-start.3
  296.3 3.9 copy-start.9
  302.0 105.0 %all-reduce.7.cloned.1.call-start = ((), (), s32[]{:S(2)}) async-start(), calls=%async_computation.7 | async-start | bytes 4194304 | tf_op jit(solution)/shard_map/psum | solution.py:12
  336.4 127.6 %reduce-scatter.5.cloned.1.call-start = ((), (), s32[]{:S(2)}) async-start(), calls=%async_computation.5 | async-start | bytes 4718592 | tf_op jit(solution)/shard_map/reduce_scatter | solution.py:66
  413.9 1.2 copy-start.12
  413.9 100.6 %reduce-scatter.3.cloned.1.call-start = ((), (), s32[]{:S(2)}) async-start(), calls=%async_computation.3 | async-start | bytes 4718592 | tf_op jit(solution)/shard_map/reduce_scatter | solution.py:66
  421.7 42.4 %copy-start.4 = (bf16[256,512]{1,0:T(8,128)(2,1)S(1)}, bf16[256,512]{1,0:T(8,128)(2,1)}, u32[]{:S(2)}) copy-start(bf16[256,512]{1,0:T(8,128)(2,1)} %convolution_convert_fusion) | copy-start | bytes 786436
  421.7 92.9 %copy-start.5 = (bf16[256,512]{1,0:T(8,128)(2,1)S(1)}, bf16[256,512]{1,0:T(8,128)(2,1)}, u32[]{:S(2)}) copy-start(bf16[256,512]{1,0:T(8,128)(2,1)} %convolution_convert_fusion.1) | copy-start | bytes 786436
  421.7 231.4 %all-reduce.5.cloned.1.call-start = ((), (), s32[]{:S(2)}) async-start(), calls=%async_computation.6 | async-start | bytes 4194304 | tf_op jit(solution)/shard_map/psum | solution.py:74
  517.8 1.0 copy-start.6
  517.8 1.2 copy-start.7
  517.8 135.3 %copy-start.1 = (f32[512,512]{1,0:T(8,128)S(1)}, f32[512,512]{1,0:T(8,128)}, u32[]{:S(2)}) copy-start(f32[512,512]{1,0:T(8,128)} %copy-done) | copy-start | bytes 3145732
Sparse Core Ops, SparseCore 0:
  154.5 31.8 all-gather.4
  302.2 31.8 all-gather.2
  337.7 69.3 all-reduce.6
  414.0 49.9 reduce-scatter.4
  466.3 48.1 reduce-scatter.2
  521.1 131.9 all-reduce.4
where the time goes:
time: 673 us; the launch traced here: 664 us
  waiting for transfers between devices  322 us (48%)
  other arithmetic  250 us (37%)
  matrix products  41.2 us (6%)
  local copies, waits for them, and re-layouts  29 us (4%)
  between operations  20.1 us (3%)
    another operation x28, other arithmetic, factor_inverse(): factor_lower = jnp.linalg.cholesky(shifted)  157 us
    psum x1, waiting for transfers between devices, local(): totals = lax.psum(jnp.stack(diagonal_terms), ('row', 'col'))  131 us
    reduce_scatter x2, waiting for transfers between devices, local(): lax.psum_scatter(product(jnp.int32(0), own_rows * lax.axis_size('col')),...  91 us
    another operation x5, other arithmetic, factor_inverse(): jax.scipy.linalg.solve_triangular(factor_lower, identity, lower=True)  78.9 us
    psum x1, waiting for transfers between devices, from_root(): return lax.psum(kept, axis)  70.3 us
    all_gather x2, waiting for transfers between devices, local(): row_block = lax.all_gather(panel_group, 'col', axis=0, tiled=True)  29.5 us
    another operation x27, local copies, waits for them, and re-layouts, factor_inverse(): jax.scipy.linalg.solve_triangular(factor_lower, identity, lower=True)  16 us
  transfers between devices with their start and end apart: 6, of which 5 were waited for; matrix products, arithmetic and copies ran while one was open for 24% of the time, Pallas kernels for 0%

commit v1 on v0

v1 whole, which is shorter than its diff:
```python
import functools

import jax
import jax.numpy as jnp
from jax import lax
from jax.experimental import pallas as pl
from jax.experimental.pallas import tpu as pltpu
from jax.sharding import PartitionSpec as P

MESH = pl.DeviceIdType.MESH
PERTURBATION = 1.0
EIG_LOW = 0.8
STEPS = 9
BF = jnp.bfloat16
F32 = jnp.float32


def split(x):
    hi = x.astype(BF)
    return hi, (x - hi.astype(F32)).astype(BF)


def dot3(a, b):
    ah, al = a
    bh, bl = b
    d = functools.partial(jnp.dot, preferred_element_type=F32)
    return d(ah, bh) + (d(ah, bl) + d(al, bh))


def eye(width):
    r = lax.broadcasted_iota(jnp.int32, (width, width), 0)
    c = lax.broadcasted_iota(jnp.int32, (width, width), 1)
    return (r == c).astype(F32)


def spread_kernel(n_row, n_col, panel, diag, flags, pc, inv, shifted, ah, al, send, recv, own):
    nodes, width = diag.shape[0], diag.shape[1]
    r, c = lax.axis_index("row"), lax.axis_index("col")
    me = r * n_col + c
    target_col = me // n_row
    slot = lax.rem(me, n_row)

    barrier = pltpu.get_barrier_semaphore()
    for j in range(n_row):
        q = c * n_row + j

        @pl.when(q != me)
        def _(q=q):
            pl.semaphore_signal(barrier, inc=1, device_id=(q // n_col, lax.rem(q, n_col)), device_id_type=MESH)

    pl.semaphore_wait(barrier, n_row - (target_col == c).astype(jnp.int32))

    def copy(dest_row, dest_slot, sem_slot):
        return pltpu.make_async_remote_copy(
            src_ref=panel,
            dst_ref=pc.at[dest_slot],
            send_sem=send.at[sem_slot],
            recv_sem=recv.at[dest_slot],
            device_id=(dest_row, target_col),
            device_id_type=MESH,
        )

    local = pltpu.make_async_copy(panel, pc.at[slot], own)
    for off in range(n_row):
        dest = lax.rem(r + off, n_row)
        is_me = jnp.logical_and(dest == r, target_col == c)

        @pl.when(is_me)
        def _():
            local.start()

        @pl.when(jnp.logical_not(is_me))
        def _(dest=dest, off=off):
            copy(dest, slot, off).start()

    low = []
    for k in range(nodes):
        a = diag[k] + PERTURBATION * eye(width) * flags[k].astype(F32)
        shifted[k] = a
        ah[k], al[k] = split(a)
        top = jnp.max(jnp.sum(jnp.abs(a), axis=0, keepdims=True), axis=1, keepdims=True)
        top = jnp.broadcast_to(top, (1, width))
        x0 = 2.0 / (EIG_LOW + top)
        low0 = EIG_LOW * x0
        grown = low0 * (2.0 - low0)
        scale = 2.0 / (1.0 + grown)
        inv[k] = (scale * x0) * (2.0 * eye(width) - x0 * a)
        low.append(scale * grown)

    def body(_, low):
        out = []
        for k in range(nodes):
            x = split(inv[k])
            rest = 2.0 * eye(width) - dot3((ah[k], al[k]), x)
            grown = low[k] * (2.0 - low[k])
            scale = 2.0 / (1.0 + grown)
            inv[k] = scale * dot3(x, split(rest))
            out.append(scale * grown)
        return tuple(out)

    lax.fori_loop(0, STEPS - 2, body, tuple(low))
    for k in range(nodes):
        x = inv[k]
        rest = eye(width) - jnp.dot(
            shifted[k], x, precision=lax.Precision.HIGHEST, preferred_element_type=F32
        )
        inv[k] = x + dot3(split(x), split(rest))

    for off in range(n_row):
        dest = lax.rem(r + off, n_row)
        is_me = jnp.logical_and(dest == r, target_col == c)

        @pl.when(is_me)
        def _():
            local.wait()

        @pl.when(jnp.logical_not(is_me))
        def _(dest=dest, off=off):
            copy(dest, slot, off).wait_send()

    for j in range(n_row):
        q = c * n_row + j

        @pl.when(q != me)
        def _(j=j):
            copy(0, j, 0).wait_recv()


def spread(n_row, n_col, panel, diag, flags):
    nodes, width = diag.shape[0], diag.shape[1]
    vm = pl.BlockSpec(memory_space=pltpu.VMEM)
    return pl.pallas_call(
        functools.partial(spread_kernel, n_row, n_col),
        out_shape=(
            jax.ShapeDtypeStruct((n_row,) + panel.shape, BF),
            jax.ShapeDtypeStruct(diag.shape, F32),
        ),
        in_specs=[vm] * 3,
        out_specs=(vm, vm),
        scratch_shapes=[
            pltpu.VMEM(diag.shape, F32),
            pltpu.VMEM(diag.shape, BF),
            pltpu.VMEM(diag.shape, BF),
            pltpu.SemaphoreType.DMA((n_row,)),
            pltpu.SemaphoreType.DMA((n_row,)),
            pltpu.SemaphoreType.DMA,
        ],
        compiler_params=pltpu.CompilerParams(
            collective_id=0, has_side_effects=True, vmem_limit_bytes=48 * 2**20
        ),
        name="spread_panels_and_invert",
    )(panel, diag, flags)


def reduce_kernel(
    n_row, n_col, part, normed, inv, panel_out, diag_out,
    pair_in, line_out, line_in, dpart, dpair, drow, dline, piece,
    pair_s, pair_r, line_s, line_r, da_s, da_r, db_s, db_r, dc_s, dc_r,
    gc_s, gc_r, gb_s, gb_r, ga_s, ga_r,
):
    nz = n_col // 2
    nodes, width = inv.shape[0], inv.shape[1]
    r, c = lax.axis_index("row"), lax.axis_index("col")
    z, core = c // 2, lax.rem(c, 2)
    other = 1 - core
    pair = (r, z * 2 + other)

    def line(off):
        zz = lax.rem(z + off, nz)
        return zz, (r, zz * 2 + core)

    def across(off):
        rr = lax.rem(r + off, n_row)
        return rr, (rr, c)

    def rc(src, dst, s, q, dev):
        return pltpu.make_async_remote_copy(
            src_ref=src, dst_ref=dst, send_sem=s, recv_sem=q, device_id=dev, device_id_type=MESH
        )

    barrier = pltpu.get_barrier_semaphore()
    pl.semaphore_signal(barrier, inc=1, device_id=pair, device_id_type=MESH)
    for off in range(1, nz):
        pl.semaphore_signal(barrier, inc=1, device_id=line(off)[1], device_id_type=MESH)
    for off in range(1, n_row):
        pl.semaphore_signal(barrier, inc=1, device_id=across(off)[1], device_id_type=MESH)
    pl.semaphore_wait(barrier, 1 + (nz - 1) + (n_row - 1))

    order = list(range(1, nz)) + [0]
    pair_copies = {}
    for off in order:
        zz, _ = line(off)
        pair_copies[off] = rc(
            part.at[zz * 2 + other], pair_in.at[off], pair_s.at[off], pair_r.at[off], pair
        )
        pair_copies[off].start()
    line_copies = {}
    for off in range(1, nz):
        zz, dev = line(off)
        pair_copies[off].wait_recv()
        line_out[off - 1] = (
            part[zz * 2 + core].astype(F32) + pair_in[off].astype(F32)
        ).astype(BF)
        line_copies[off] = rc(
            line_out.at[off - 1], line_in.at[off - 1], line_s.at[off - 1], line_r.at[off - 1], dev
        )
        line_copies[off].start()
    pair_copies[0].wait_recv()
    for off in range(1, nz):
        line_copies[off].wait_recv()

    for k in range(nodes):
        cols = pl.ds(k * width, width)
        applied = part[c, :, cols].astype(F32) + pair_in[0, :, cols].astype(F32)
        for off in range(1, nz):
            applied = applied + line_in[off - 1, :, cols].astype(F32)
        panel_out[k] = (-applied).astype(BF)
        hi, lo = split(applied)
        left = normed[:, cols]
        dims = (((0,), (0,)), ((), ()))
        dpart[k] = lax.dot_general(left, hi, dims, preferred_element_type=F32) + lax.dot_general(
            left, lo, dims, preferred_element_type=F32
        )

    half = nodes // 2
    first = core * half
    hold = pl.ds(first, half)
    copy = rc(dpart.at[pl.ds(other * half, half)], dpair, da_s.at[0], da_r.at[0], pair)
    copy.start()
    copy.wait_recv()
    dpart[hold] = dpart[hold] + dpair[...]
    copies = [copy]

    rows_b = width // n_row
    stage = []
    for off in range(1, n_row):
        rr, dev = across(off)
        cp = rc(
            dpart.at[hold, pl.ds(rr * rows_b, rows_b)],
            drow.at[off - 1], db_s.at[off - 1], db_r.at[off - 1], dev,
        )
        cp.start()
        stage.append(cp)
    start_b = pl.multiple_of(r * rows_b, rows_b)
    for cp in stage:
        cp.wait_recv()
    total = dpart[hold, pl.ds(start_b, rows_b)]
    for off in range(1, n_row):
        total = total + drow[off - 1]
    piece[...] = total
    copies += stage

    rows_c = rows_b // nz
    stage = []
    for off in range(1, nz):
        zz, dev = line(off)
        cp = rc(
            piece.at[:, pl.ds(zz * rows_c, rows_c)],
            dline.at[off - 1], dc_s.at[off - 1], dc_r.at[off - 1], dev,
        )
        cp.start()
        stage.append(cp)
    start_c = pl.multiple_of(z * rows_c, rows_c)
    for cp in stage:
        cp.wait_recv()
    total = piece[:, pl.ds(start_c, rows_c)]
    for off in range(1, nz):
        total = total + dline[off - 1]
    mine = pl.multiple_of(start_b + start_c, rows_c)
    diag_out[hold, pl.ds(mine, rows_c)] = total + inv[hold, pl.ds(mine, rows_c)]
    copies += stage

    stage = []
    for off in range(1, nz):
        _, dev = line(off)
        at = diag_out.at[hold, pl.ds(mine, rows_c)]
        cp = rc(at, at, gc_s.at[off - 1], gc_r.at[off - 1], dev)
        cp.start()
        stage.append(cp)
    for cp in stage:
        cp.wait_recv()
    copies += stage
    stage = []
    for off in range(1, n_row):
        _, dev = across(off)
        at = diag_out.at[hold, pl.ds(start_b, rows_b)]
        cp = rc(at, at, gb_s.at[off - 1], gb_r.at[off - 1], dev)
        cp.start()
        stage.append(cp)
    for cp in stage:
        cp.wait_recv()
    copies += stage
    at = diag_out.at[hold]
    cp = rc(at, at, ga_s.at[0], ga_r.at[0], pair)
    cp.start()
    cp.wait_recv()
    copies.append(cp)
    for off in order:
        pair_copies[off].wait_send()
    for off in range(1, nz):
        line_copies[off].wait_send()
    for cp in copies:
        cp.wait_send()


def reduce(n_row, n_col, part, normed, inv):
    nz = n_col // 2
    nodes, width = inv.shape[0], inv.shape[1]
    rows = normed.shape[0]
    half = nodes // 2
    rows_b = width // n_row
    rows_c = rows_b // nz
    vm = pl.BlockSpec(memory_space=pltpu.VMEM)
    dma = pltpu.SemaphoreType.DMA
    return pl.pallas_call(
        functools.partial(reduce_kernel, n_row, n_col),
        out_shape=(
            jax.ShapeDtypeStruct((nodes, rows, width), BF),
            jax.ShapeDtypeStruct(inv.shape, F32),
        ),
        in_specs=[vm] * 3,
        out_specs=(vm, vm),
        scratch_shapes=[
            pltpu.VMEM((nz, rows, nodes * width), BF),
            pltpu.VMEM((nz - 1, rows, nodes * width), BF),
            pltpu.VMEM((nz - 1, rows, nodes * width), BF),
            pltpu.VMEM(inv.shape, F32),
            pltpu.VMEM((half, width, width), F32),
            pltpu.VMEM((n_row - 1, half, rows_b, width), F32),
            pltpu.VMEM((nz - 1, half, rows_c, width), F32),
            pltpu.VMEM((half, rows_b, width), F32),
            dma((nz,)), dma((nz,)), dma((nz - 1,)), dma((nz - 1,)),
            dma((1,)), dma((1,)), dma((n_row - 1,)), dma((n_row - 1,)),
            dma((nz - 1,)), dma((nz - 1,)), dma((nz - 1,)), dma((nz - 1,)),
            dma((n_row - 1,)), dma((n_row - 1,)), dma((1,)), dma((1,)),
        ],
        compiler_params=pltpu.CompilerParams(
            collective_id=1, has_side_effects=True, vmem_limit_bytes=48 * 2**20
        ),
        name="sum_products_and_diagonals",
    )(part, normed, inv)


def normalize(rows, inv):
    hi, lo = split(inv)
    dims = (((2,), (1,)), ((0,), (0,)))
    d = functools.partial(lax.dot_general, dimension_numbers=dims, preferred_element_type=F32)
    return (d(rows, hi) + d(rows, lo)).astype(BF)


def local(n_row, n_col, diag_blocks, pivot_flags, panels, structure, ancestor_inverse):
    nodes, rows, width = panels.shape
    masked = panels * structure.astype(BF)[:, :, None]
    column, inv = spread(n_row, n_col, masked, diag_blocks, pivot_flags[:, None, :])
    column = column.transpose(1, 0, 2, 3).reshape(nodes, n_row * rows, width)
    block = normalize(column, inv).transpose(1, 0, 2).reshape(n_row * rows, nodes * width)
    own = normalize(masked, inv).transpose(1, 0, 2).reshape(rows, nodes * width)
    part = jnp.dot(ancestor_inverse, block, preferred_element_type=F32).astype(BF)
    part = part.reshape(n_col, rows, nodes * width)
    return reduce(n_row, n_col, part, own, inv)


def solution(mesh):
    in_specs = (P(), P(), P(None, ("row", "col"), None), P(None, ("row", "col")), P("row", "col"))
    out_specs = (P(None, ("row", "col"), None), P())
    body = functools.partial(local, mesh.shape["row"], mesh.shape["col"])
    return jax.shard_map(body, mesh=mesh, in_specs=in_specs, out_specs=out_specs, check_vma=False)
```

time: 673 us -> 258 us (0.38); the launches traced: 664 us -> 258 us
  waiting for transfers between devices: 322 us -> 0 us
  other arithmetic: 250 us -> 1.86 us
  Pallas kernels: 0 us -> 235 us
  matrix products: 41.2 us -> 9.57 us
  between operations: 20.1 us -> 0.71 us
  local copies, waits for them, and re-layouts: 29 us -> 10.3 us
    another operation x34 -> x0, other arithmetic: 238 us -> none  [the longest x28 157 us: factor_inverse(): factor_lower = jnp.linalg.cholesky(shifted)]
    pallas_call x0 -> x2, Pallas kernels: none -> 235 us  [the longest x1 126 us: reduce(): pl.pallas_call(functools.partial(reduce_kernel, n_row, n_col), out_shape=...]
    psum x2 -> x0, waiting for transfers between devices: 202 us -> none  [the longest x1 131 us: local(): totals = lax.psum(jnp.stack(diagonal_terms), ('row', 'col'))]
    reduce_scatter x2 -> x0, waiting for transfers between devices: 91 us -> none  [local(): lax.psum_scatter(product(jnp.int32(0), own_rows * lax.axis_size('col')),...]
    all_gather x2 -> x0, waiting for transfers between devices: 29.5 us -> none  [local(): row_block = lax.all_gather(panel_group, 'col', axis=0, tiled=True)]
    another operation x26 -> x0, matrix products: 16.9 us -> none  [the longest x14 9.54 us: factor_inverse(): jax.scipy.linalg.solve_triangular(factor_lower, identity, lower=True)]
    another operation x35 -> x0, local copies, waits for them, and re-layouts: 16.3 us -> none  [the longest x27 16 us: factor_inverse(): jax.scipy.linalg.solve_triangular(factor_lower, identity, lower=True)]
    dot_general x8 -> x5, matrix products: 24.3 us -> 9.57 us  [the longest x1 6.09 us: local(): jnp.dot(ancestor_inverse, block, preferred_element_type=F32).astype(BF)]
  transfers between devices with their start and end apart: 6 -> 0, of which waited for: 5 -> 0; matrix products, arithmetic and copies ran while one was open for 24% -> 0% of each run, Pallas kernels for 0% -> 0%
where the time goes in v1:
time: 258 us
  Pallas kernels  235 us (91%)
  local copies, waits for them, and re-layouts  10.3 us (4%)
  matrix products  9.57 us (4%)
    pallas_call x1, Pallas kernels, reduce(): pl.pallas_call(functools.partial(reduce_kernel, n_row, n_col), out_shape=...  126 us
    pallas_call x1, Pallas kernels, spread(): pl.pallas_call(functools.partial(spread_kernel, n_row, n_col), out_shape=...  110 us
    convert_element_type x1, local copies, waits for them, and re-layouts, local(): jnp.dot(ancestor_inverse, block, preferred_element_type=F32).astype(BF)  6.42 us
    dot_general x1, matrix products, local(): jnp.dot(ancestor_inverse, block, preferred_element_type=F32).astype(BF)  6.09 us

profile of v1, /device:TPU:0, one launch (start us, length us, event | category | flops | bytes accessed | tf_op | source)
XLA Modules:
  0.0 257.7 jit_solution(10646535458975385396)
XLA Ops:
  0.6 0.7 convert_element_type.35
  1.3 0.7 broadcast_in_dim.4.flags
  2.0 1.2 broadcast_multiply_fusion.panel
  3.2 109.5 %spread_panels_and_invert.1 = (bf16[4,2,256,512]{3,2,1,0:T(8,128)(2,1)S(1)}, f32[2,512,512]{2,1,0:T(8,128)S(1)}) custom-call(bf16[2,256,512]{2,1,0:T(8,128)(2,1)S(1)} %broadcast_multiply_fusion.panel, f32[2,512,512]{2,1,0:T(8,128)} %diag.1, s32[2,1,512]{2,1,0:T(1,128)S(1)} %broadcast_in_dim.4.flags), custom_call_target="tpu_custom_call" | custom-call | tf_op jit(solution)/shard_map/spread_panels_and_invert/pallas_call | solution.py:132
  112.7 0.1 copy.11
  112.9 0.4 fusion.2
  113.3 0.4 fusion.1
  113.8 0.1 copy.18
  113.8 1.3 fusion.4
  115.1 0.0 copy-start
  115.2 1.3 add_convert_fusion
  116.5 0.9 copy-done
  117.3 6.1 %convert_bitcast_fusion = bf16[2048,1024]{0,1:T(8,128)(2,1)} fusion(bf16[1024,1024]{0,1:T(8,128)(2,1)S(1)} %bitcast.23, bf16[2048,1024]{1,0:T(8,128)(2,1)S(1)} %copy-done), kind=kOutput, calls=%fused_computation | convolution fusion | flops 4297064448 | bytes 10485760 | tf_op jit(solution)/shard_map/dot_general | solution.py:358
  123.4 6.4 %copy.14 = bf16[2048,1024]{1,0:T(8,128)(2,1)} copy(bf16[2048,1024]{0,1:T(8,128)(2,1)} %convert_bitcast_fusion) | data formatting | bytes 8388608 | tf_op jit(solution)/shard_map/convert_element_type | solution.py:358
  129.8 125.8 %sum_products_and_diagonals.1 = (bf16[2,256,512]{2,1,0:T(8,128)(2,1)S(1)}, f32[2,512,512]{2,1,0:T(8,128)S(1)}) custom-call(bf16[8,256,1024]{2,1,0:T(8,128)(2,1)} %bitcast.22, bf16[256,1024]{1,0:T(8,128)(2,1)S(1)} %bitcast.19, f32[2,512,512]{2,1,0:T(8,128)S(1)} %get-tuple-element.5.inv), custom_call_target="tpu_custom_call" | custom-call | tf_op jit(solution)/shard_map/sum_products_and_diagonals/pallas_call | solution.py:315
  255.6 0.8 copy.21
  256.4 1.3 copy.22
Async XLA Ops:
  115.1 2.2 copy-start

commit v2 on v1

--- a/solution.py
+++ b/solution.py
@@ -33,51 +33,95 @@
     return (r == c).astype(F32)
 
 
-def spread_kernel(n_row, n_col, panel, diag, flags, pc, inv, shifted, ah, al, send, recv, own):
+def spread_kernel(
+    n_row, n_col, panel, diag, flags, pc, inv, held, shifted, ah, al,
+    s1, r1, s2, r2, s3, r3, sx, rx,
+):
     nodes, width = diag.shape[0], diag.shape[1]
+    ratio = n_col // n_row
+    half = nodes // 2
     r, c = lax.axis_index("row"), lax.axis_index("col")
-    me = r * n_col + c
-    target_col = me // n_row
-    slot = lax.rem(me, n_row)
+    core = lax.rem(c, 2)
+    pair = (r, c + 1 - 2 * core)
+    slot = lax.rem(c, n_row)
+    count = panel.shape[1] // n_row
+
+    def rows(i):
+        return pl.ds(pl.multiple_of(i * count, count), count)
+
+    def goal(row):
+        return row * ratio + c // n_row
+
+    def across(off):
+        return lax.rem(r + off, n_row)
+
+    def rc(src, dst, s, q, dev):
+        return pltpu.make_async_remote_copy(
+            src_ref=src, dst_ref=dst, send_sem=s, recv_sem=q, device_id=dev, device_id_type=MESH
+        )
 
     barrier = pltpu.get_barrier_semaphore()
+    pl.semaphore_signal(barrier, inc=1, device_id=pair, device_id_type=MESH)
+    expect = n_row
+    for off in range(1, n_row):
+        pl.semaphore_signal(barrier, inc=1, device_id=(across(off), c), device_id_type=MESH)
     for j in range(n_row):
-        q = c * n_row + j
-
-        @pl.when(q != me)
-        def _(q=q):
-            pl.semaphore_signal(barrier, inc=1, device_id=(q // n_col, lax.rem(q, n_col)), device_id_type=MESH)
-
-    pl.semaphore_wait(barrier, n_row - (target_col == c).astype(jnp.int32))
-
-    def copy(dest_row, dest_slot, sem_slot):
-        return pltpu.make_async_remote_copy(
-            src_ref=panel,
-            dst_ref=pc.at[dest_slot],
-            send_sem=send.at[sem_slot],
-            recv_sem=recv.at[dest_slot],
-            device_id=(dest_row, target_col),
-            device_id_type=MESH,
-        )
-
-    local = pltpu.make_async_copy(panel, pc.at[slot], own)
-    for off in range(n_row):
-        dest = lax.rem(r + off, n_row)
-        is_me = jnp.logical_and(dest == r, target_col == c)
-
-        @pl.when(is_me)
-        def _():
-            local.start()
-
-        @pl.when(jnp.logical_not(is_me))
-        def _(dest=dest, off=off):
-            copy(dest, slot, off).start()
+        sender = lax.rem(n_row * c + j, n_col)
+
+        @pl.when(sender != c)
+        def _(sender=sender):
+            pl.semaphore_signal(barrier, inc=1, device_id=(r, sender), device_id_type=MESH)
+
+        expect = expect + (goal(j) != c).astype(jnp.int32)
+    pl.semaphore_wait(barrier, expect)
+
+    first = []
+    for off in range(1, n_row):
+        to = across(off)
+        cp = rc(panel.at[:, rows(to)], held.at[r], s1.at[off - 1], r1.at[off - 1], (to, c))
+        cp.start()
+        first.append(cp)
+    held[r] = panel[:, rows(r)]
+
+    def second(j):
+        return rc(held.at[j], pc.at[slot, :, rows(r)], s2.at[j], r2.at[slot], (r, goal(j)))
+
+    def forward():
+        for cp in first:
+            cp.wait_recv()
+        for j in range(n_row):
+
+            @pl.when(goal(j) != c)
+            def _(j=j):
+                second(j).start()
+
+            @pl.when(goal(j) == c)
+            def _(j=j):
+                pc[slot, :, rows(r)] = held[j]
+
+    third = []
+
+    def gather():
+        for j in range(n_row):
+            sender = lax.rem(n_row * c + j, n_col)
+
+            @pl.when(sender != c)
+            def _(j=j):
+                at = pc.at[j, :, rows(r)]
+                rc(held.at[0], at, s2.at[0], r2.at[j], pair).wait_recv()
+
+            at = pc.at[j, :, rows(r)]
+            for off in range(1, n_row):
+                cp = rc(at, at, s3.at[off - 1, j], r3.at[off - 1, j], (across(off), c))
+                cp.start()
+                third.append(cp)
 
     low = []
-    for k in range(nodes):
+    for i in range(half):
+        k = core * half + i
         a = diag[k] + PERTURBATION * eye(width) * flags[k].astype(F32)
-        shifted[k] = a
-        ah[k], al[k] = split(a)
+        shifted[i] = a
+        ah[i], al[i] = split(a)
         top = jnp.max(jnp.sum(jnp.abs(a), axis=0, keepdims=True), axis=1, keepdims=True)
         top = jnp.broadcast_to(top, (1, width))
         x0 = 2.0 / (EIG_LOW + top)
@@ -89,46 +133,49 @@
 
     def body(_, low):
         out = []
-        for k in range(nodes):
+        for i in range(half):
+            k = core * half + i
             x = split(inv[k])
-            rest = 2.0 * eye(width) - dot3((ah[k], al[k]), x)
-            grown = low[k] * (2.0 - low[k])
+            rest = 2.0 * eye(width) - dot3((ah[i], al[i]), x)
+            grown = low[i] * (2.0 - low[i])
             scale = 2.0 / (1.0 + grown)
             inv[k] = scale * dot3(x, split(rest))
             out.append(scale * grown)
         return tuple(out)
 
-    lax.fori_loop(0, STEPS - 2, body, tuple(low))
-    for k in range(nodes):
+    low = lax.fori_loop(0, 2, body, tuple(low))
+    forward()
+    low = lax.fori_loop(0, 3, body, low)
+    gather()
+    lax.fori_loop(0, STEPS - 7, body, low)
+    for i in range(half):
+        k = core * half + i
         x = inv[k]
         rest = eye(width) - jnp.dot(
-            shifted[k], x, precision=lax.Precision.HIGHEST, preferred_element_type=F32
+            shifted[i], x, precision=lax.Precision.HIGHEST, preferred_element_type=F32
         )
         inv[k] = x + dot3(split(x), split(rest))
-
-    for off in range(n_row):
-        dest = lax.rem(r + off, n_row)
-        is_me = jnp.logical_and(dest == r, target_col == c)
-
-        @pl.when(is_me)
-        def _():
-            local.wait()
-
-        @pl.when(jnp.logical_not(is_me))
-        def _(dest=dest, off=off):
-            copy(dest, slot, off).wait_send()
-
+    at = inv.at[pl.ds(core * half, half)]
+    swap = rc(at, at, sx.at[0], rx.at[0], pair)
+    swap.start()
+    swap.wait_recv()
+    for cp in third:
+        cp.wait_recv()
+    swap.wait_send()
+    for cp in first + third:
+        cp.wait_send()
     for j in range(n_row):
-        q = c * n_row + j
-
-        @pl.when(q != me)
+
+        @pl.when(goal(j) != c)
         def _(j=j):
-            copy(0, j, 0).wait_recv()
+            second(j).wait_send()
 
 
 def spread(n_row, n_col, panel, diag, flags):
     nodes, width = diag.shape[0], diag.shape[1]
     vm = pl.BlockSpec(memory_space=pltpu.VMEM)
+    dma = pltpu.SemaphoreType.DMA
+    some = (nodes // 2,) + diag.shape[1:]
     return pl.pallas_call(
         functools.partial(spread_kernel, n_row, n_col),
         out_shape=(
@@ -138,12 +185,14 @@
         in_specs=[vm] * 3,
         out_specs=(vm, vm),
         scratch_shapes=[
-            pltpu.VMEM(diag.shape, F32),
-            pltpu.VMEM(diag.shape, BF),
-            pltpu.VMEM(diag.shape, BF),
-            pltpu.SemaphoreType.DMA((n_row,)),
-            pltpu.SemaphoreType.DMA((n_row,)),
-            pltpu.SemaphoreType.DMA,
+            pltpu.VMEM((n_row, nodes, panel.shape[1] // n_row, width), BF),
+            pltpu.VMEM(some, F32),
+            pltpu.VMEM(some, BF),
+            pltpu.VMEM(some, BF),
+            dma((n_row - 1,)), dma((n_row - 1,)),
+            dma((n_row,)), dma((n_row,)),
+            dma((n_row - 1, n_row)), dma((n_row - 1, n_row)),
+            dma((1,)), dma((1,)),
         ],
         compiler_params=pltpu.CompilerParams(
             collective_id=0, has_side_effects=True, vmem_limit_bytes=48 * 2**20

time: 258 us -> 164 us (0.64)
  Pallas kernels: 235 us -> 140 us
    pallas_call x1, Pallas kernels: 110 us -> 43.8 us  [spread(): pl.pallas_call(functools.partial(spread_kernel, n_row, n_col), out_shape=...]
    pallas_call x1, Pallas kernels: 126 us -> 96.2 us  [reduce(): pl.pallas_call(functools.partial(reduce_kernel, n_row, n_col), out_shape=...]
where the time goes in v2:
time: 164 us; the launch traced here: 162 us
  Pallas kernels  140 us (85%)
  local copies, waits for them, and re-layouts  10.3 us (6%)
  matrix products  9.57 us (6%)
  other arithmetic  1.86 us (1%)
    pallas_call x1, Pallas kernels, reduce(): pl.pallas_call(functools.partial(reduce_kernel, n_row, n_col), out_shape=...  96.2 us
    pallas_call x1, Pallas kernels, spread(): pl.pallas_call(functools.partial(spread_kernel, n_row, n_col), out_shape=...  43.8 us
    convert_element_type x1, local copies, waits for them, and re-layouts, local(): jnp.dot(ancestor_inverse, block, preferred_element_type=F32).astype(BF)  6.42 us
    dot_general x1, matrix products, local(): jnp.dot(ancestor_inverse, block, preferred_element_type=F32).astype(BF)  6.09 us
    dot_general x4, matrix products, normalize(): return (d(rows, hi) + d(rows, lo)).astype(BF)  3.48 us

profile of v2, /device:TPU:0, one launch (start us, length us, event | category | flops | bytes accessed | tf_op | source)
XLA Modules:
  0.0 162.4 jit_solution(9721869880087561932)
XLA Ops:
  0.6 0.7 convert_element_type.35
  1.3 0.7 broadcast_in_dim.4.flags
  2.0 1.2 broadcast_multiply_fusion.panel
  3.2 43.8 %spread_panels_and_invert.1 = (bf16[4,2,256,512]{3,2,1,0:T(8,128)(2,1)S(1)}, f32[2,512,512]{2,1,0:T(8,128)S(1)}) custom-call(bf16[2,256,512]{2,1,0:T(8,128)(2,1)S(1)} %broadcast_multiply_fusion.panel, f32[2,512,512]{2,1,0:T(8,128)} %diag.1, s32[2,1,512]{2,1,0:T(1,128)S(1)} %broadcast_in_dim.4.flags), custom_call_target="tpu_custom_call" | custom-call | tf_op jit(solution)/shard_map/spread_panels_and_invert/pallas_call | solution.py:179
  46.9 0.1 copy.11
  47.1 0.4 fusion.2
  47.5 0.4 fusion.1
  48.0 0.1 copy.18
  48.1 1.3 fusion.4
  49.4 0.0 copy-start
  49.4 1.3 add_convert_fusion
  50.7 0.9 copy-done
  51.6 6.1 %convert_bitcast_fusion = bf16[2048,1024]{0,1:T(8,128)(2,1)} fusion(bf16[1024,1024]{0,1:T(8,128)(2,1)S(1)} %bitcast.23, bf16[2048,1024]{1,0:T(8,128)(2,1)S(1)} %copy-done), kind=kOutput, calls=%fused_computation | convolution fusion | flops 4297064448 | bytes 10485760 | tf_op jit(solution)/shard_map/dot_general | solution.py:407
  57.6 6.4 %copy.14 = bf16[2048,1024]{1,0:T(8,128)(2,1)} copy(bf16[2048,1024]{0,1:T(8,128)(2,1)} %convert_bitcast_fusion) | data formatting | bytes 8388608 | tf_op jit(solution)/shard_map/convert_element_type | solution.py:407
  64.1 96.2 %sum_products_and_diagonals.1 = (bf16[2,256,512]{2,1,0:T(8,128)(2,1)S(1)}, f32[2,512,512]{2,1,0:T(8,128)S(1)}) custom-call(bf16[8,256,1024]{2,1,0:T(8,128)(2,1)} %bitcast.22, bf16[256,1024]{1,0:T(8,128)(2,1)S(1)} %bitcast.19, f32[2,512,512]{2,1,0:T(8,128)S(1)} %get-tuple-element.5.inv), custom_call_target="tpu_custom_call" | custom-call | tf_op jit(solution)/shard_map/sum_products_and_diagonals/pallas_call | solution.py:364
  160.3 0.8 copy.21
  161.0 1.3 copy.22
Async XLA Ops:
  49.4 2.2 %copy-start = (bf16[2048,1024]{1,0:T(8,128)(2,1)S(1)}, bf16[2048,1024]{1,0:T(8,128)(2,1)}, u32[]{:S(2)}) copy-start(bf16[2048,1024]{1,0:T(8,128)(2,1)} %param.9) | copy-start | bytes 12582916

commit v3 on v2

--- a/solution.py
+++ b/solution.py
@@ -202,8 +202,8 @@
 
 
 def reduce_kernel(
-    n_row, n_col, part, normed, inv, panel_out, diag_out,
-    pair_in, line_out, line_in, dpart, dpair, drow, dline, piece,
+    n_row, n_col, tile, block, normed, inv, panel_out, diag_out,
+    pair_out, own, pair_in, line_out, line_in, dpart, dpair, drow, dline, piece,
     pair_s, pair_r, line_s, line_r, da_s, da_r, db_s, db_r, dc_s, dc_r,
     gc_s, gc_r, gb_s, gb_r, ga_s, ga_r,
 ):
@@ -235,32 +235,41 @@
         pl.semaphore_signal(barrier, inc=1, device_id=across(off)[1], device_id_type=MESH)
     pl.semaphore_wait(barrier, 1 + (nz - 1) + (n_row - 1))
 
+    count = normed.shape[0]
     order = list(range(1, nz)) + [0]
     pair_copies = {}
-    for off in order:
+    line_copies = {}
+
+    def product(index):
+        at = pl.ds(pl.multiple_of(index * count, count), count)
+        return jnp.dot(tile[at, :], block[...], preferred_element_type=F32)
+
+    def to_pair(off):
         zz, _ = line(off)
-        pair_copies[off] = rc(
-            part.at[zz * 2 + other], pair_in.at[off], pair_s.at[off], pair_r.at[off], pair
-        )
+        pair_out[off] = product(zz * 2 + other).astype(BF)
+        pair_copies[off] = rc(pair_out.at[off], pair_in.at[off], pair_s.at[off], pair_r.at[off], pair)
         pair_copies[off].start()
-    line_copies = {}
-    for off in range(1, nz):
+
+    to_pair(order[0])
+    for step, off in enumerate(order):
+        if step + 1 < nz:
+            to_pair(order[step + 1])
         zz, dev = line(off)
+        own[...] = product(zz * 2 + core)
         pair_copies[off].wait_recv()
-        line_out[off - 1] = (
-            part[zz * 2 + core].astype(F32) + pair_in[off].astype(F32)
-        ).astype(BF)
+        if off == 0:
+            continue
+        line_out[off - 1] = (own[...] + pair_in[off].astype(F32)).astype(BF)
         line_copies[off] = rc(
             line_out.at[off - 1], line_in.at[off - 1], line_s.at[off - 1], line_r.at[off - 1], dev
         )
         line_copies[off].start()
-    pair_copies[0].wait_recv()
     for off in range(1, nz):
         line_copies[off].wait_recv()
 
     for k in range(nodes):
         cols = pl.ds(k * width, width)
-        applied = part[c, :, cols].astype(F32) + pair_in[0, :, cols].astype(F32)
+        applied = own[:, cols] + pair_in[0, :, cols].astype(F32)
         for off in range(1, nz):
             applied = applied + line_in[off - 1, :, cols].astype(F32)
         panel_out[k] = (-applied).astype(BF)
@@ -352,7 +361,7 @@
         cp.wait_send()
 
 
-def reduce(n_row, n_col, part, normed, inv):
+def reduce(n_row, n_col, tile, block, normed, inv):
     nz = n_col // 2
     nodes, width = inv.shape[0], inv.shape[1]
     rows = normed.shape[0]
@@ -367,9 +376,11 @@
             jax.ShapeDtypeStruct((nodes, rows, width), BF),
             jax.ShapeDtypeStruct(inv.shape, F32),
         ),
-        in_specs=[vm] * 3,
+        in_specs=[vm] * 4,
         out_specs=(vm, vm),
         scratch_shapes=[
+            pltpu.VMEM((nz, rows, nodes * width), BF),
+            pltpu.VMEM((rows, nodes * width), F32),
             pltpu.VMEM((nz, rows, nodes * width), BF),
             pltpu.VMEM((nz - 1, rows, nodes * width), BF),
             pltpu.VMEM((nz - 1, rows, nodes * width), BF),
@@ -384,10 +395,10 @@
             dma((n_row - 1,)), dma((n_row - 1,)), dma((1,)), dma((1,)),
         ],
         compiler_params=pltpu.CompilerParams(
-            collective_id=1, has_side_effects=True, vmem_limit_bytes=48 * 2**20
+            collective_id=1, has_side_effects=True, vmem_limit_bytes=58 * 2**20
         ),
         name="sum_products_and_diagonals",
-    )(part, normed, inv)
+    )(tile, block, normed, inv)
 
 
 def normalize(rows, inv):
@@ -404,9 +415,7 @@
     column = column.transpose(1, 0, 2, 3).reshape(nodes, n_row * rows, width)
     block = normalize(column, inv).transpose(1, 0, 2).reshape(n_row * rows, nodes * width)
     own = normalize(masked, inv).transpose(1, 0, 2).reshape(rows, nodes * width)
-    part = jnp.dot(ancestor_inverse, block, preferred_element_type=F32).astype(BF)
-    part = part.reshape(n_col, rows, nodes * width)
-    return reduce(n_row, n_col, part, own, inv)
+    return reduce(n_row, n_col, ancestor_inverse, block, own, inv)
 
 
 def solution(mesh):

time: 164 us -> 162 us (0.988)
  matrix products: 9.57 us -> 3.51 us
  Pallas kernels: 140 us -> 146 us
    pallas_call x1, Pallas kernels: 96.2 us -> 103 us  [reduce(): pl.pallas_call(functools.partial(reduce_kernel, n_row, n_col), out_shape=...]
    convert_element_type x1 -> x0, local copies, waits for them, and re-layouts: 6.42 us -> none  [local(): jnp.dot(ancestor_inverse, block, preferred_element_type=F32).astype(BF)]
    dot_general x1 -> x0, matrix products: 6.09 us -> none  [local(): jnp.dot(ancestor_inverse, block, preferred_element_type=F32).astype(BF)]
    reshape x0 -> x1, local copies, waits for them, and re-layouts: none -> 2.56 us  [local(): normalize(column, inv).transpose(1, 0, 2)]
    unnamed x4, local copies, waits for them, and re-layouts: 2.99 us -> 4.95 us
where the time goes in v3:
time: 162 us
  Pallas kernels  146 us (90%)
  local copies, waits for them, and re-layouts  9.29 us (6%)
  matrix products  3.51 us (2%)
  other arithmetic  1.86 us (1%)
    pallas_call x1, Pallas kernels, reduce(): pl.pallas_call(functools.partial(reduce_kernel, n_row, n_col), out_shape=...  103 us
    pallas_call x1, Pallas kernels, spread(): pl.pallas_call(functools.partial(spread_kernel, n_row, n_col), out_shape=...  43.7 us
    unnamed x4, local copies, waits for them, and re-layouts  4.95 us
    dot_general x4, matrix products, normalize(): return (d(rows, hi) + d(rows, lo)).astype(BF)  3.51 us

profile of v3, /device:TPU:0, one launch (start us, length us, event | category | flops | bytes accessed | tf_op | source)
XLA Modules:
  0.0 161.8 jit_solution(2029326925939893012)
XLA Ops:
  0.6 0.7 convert_element_type.29
  1.3 0.7 broadcast_in_dim.4.flags
  2.0 1.2 broadcast_multiply_fusion.panel
  3.2 43.7 %spread_panels_and_invert.1 = (bf16[4,2,256,512]{3,2,1,0:T(8,128)(2,1)S(1)}, f32[2,512,512]{2,1,0:T(8,128)S(1)}) custom-call(bf16[2,256,512]{2,1,0:T(8,128)(2,1)S(1)} %broadcast_multiply_fusion.panel, f32[2,512,512]{2,1,0:T(8,128)} %diag.1, s32[2,1,512]{2,1,0:T(1,128)S(1)} %broadcast_in_dim.4.flags), custom_call_target="tpu_custom_call" | custom-call | tf_op jit(solution)/shard_map/spread_panels_and_invert/pallas_call | solution.py:179
  46.9 0.0 copy-start
  46.9 0.2 copy.11
  47.2 0.4 fusion.2
  47.6 0.4 fusion.1
  48.1 0.9 copy.19
  48.9 1.3 fusion.4
  50.2 0.0 copy-done
  50.2 1.3 add_convert_fusion
  51.6 2.6 %copy.18.block = bf16[1024,1024]{1,0:T(8,128)(2,1)} copy(bf16[1024,1024]{0,1:T(8,128)(2,1)S(1)} %bitcast.16) | data formatting | bytes 4194304 | tf_op jit(solution)/shard_map/reshape | solution.py:416
  54.1 102.6 %sum_products_and_diagonals.1 = (bf16[2,256,512]{2,1,0:T(8,128)(2,1)}, f32[2,512,512]{2,1,0:T(8,128)}) custom-call(bf16[2048,1024]{1,0:T(8,128)(2,1)} %tile.1, bf16[1024,1024]{1,0:T(8,128)(2,1)} %copy.18.block, bf16[256,1024]{1,0:T(8,128)(2,1)} %bitcast.17, f32[2,512,512]{2,1,0:T(8,128)} %copy-done), custom_call_target="tpu_custom_call" | custom-call | tf_op jit(solution)/shard_map/sum_products_and_diagonals/pallas_call | solution.py:373
  156.8 1.9 %copy.22 = bf16[2,256,512]{2,1,0:T(8,128)(2,1)} copy(bf16[2,256,512]{2,1,0:T(8,128)(2,1)} %get-tuple-element.8) | data formatting | bytes 1048576
  158.7 3.1 %copy.23 = f32[2,512,512]{2,1,0:T(8,128)} copy(f32[2,512,512]{2,1,0:T(8,128)} %get-tuple-element.9) | data formatting | bytes 4194304
Async XLA Ops:
  46.9 3.3 %copy-start = (f32[2,512,512]{2,1,0:T(8,128)}, f32[2,512,512]{2,1,0:T(8,128)S(1)}, u32[]{:S(2)}) copy-start(f32[2,512,512]{2,1,0:T(8,128)S(1)} %get-tuple-element.5.inv) | copy-start | bytes 6291460
